TPU v7x, 512 devices: a whole 4x4x16 slice. The times are simulated.
512 devices in a mesh: face: 8 (over x, y_lo), tile: 64 (over z, y_hi, core).
Axes of the slice: x: 4, y: 4 (y_hi: 2, y_lo: 2; y = y_hi * 2 + y_lo), z: 16, core: 2. Of those that a mesh axis runs over, the one named last changes fastest.
Arguments:
- maps: bfloat16 [4, 4, 128, 8192], P(None, None, 'face', 'tile'), may hold values from -8 to 8
- params: float32 [4, 2], replicated, may hold values from 0 to 1
- labels: int32 [4], replicated, may hold values 0 or 1
- edge_flip: int32 [8, 64], replicated, may hold values from 0 to 1
- fine_weight: float32 [3, 4, 16], replicated, may hold values from -1.75 to 1.75
- coarse_weight: float32 [3, 16, 32], replicated, may hold values from -0.875 to 0.875
- feature_weight: float32 [32, 128], replicated, may hold values from -2 to 2
- param_weight: float32 [2, 128], replicated, may hold values from -4 to 4
- out_weight: float32 [128], replicated, may hold values from -1 to 1
Outputs:
- logits: float32 [4], replicated
- saliency: float32 [4, 4, 128, 8192], P(None, None, 'face', 'tile')
- grad_fine: float32 [3, 4, 16], replicated
- grad_coarse: float32 [3, 16, 32], replicated
All inputs are finite; a program needn't handle non-finite values.
Results may differ from a plain program's by a relative error of at most 0.0003.
Values sent between devices are 32-bit elements; how exact they have to be, the bound alone decides.
No kernel may reach another device: no remote copies, remote signals or barrier semaphores. Data moves between devices by JAX's collectives and lax.ppermute only.
A program may use at most 64 MiB of HBM per device.

v0:
```python
import jax
import jax.numpy as jnp
from jax import lax
from jax.sharding import PartitionSpec as P

exact = lax.Precision.HIGHEST


def with_halo(block, sides, width):
    for axis, dim in sides:
        count = lax.axis_size(axis)
        forward = [(i, i + 1) for i in range(count - 1)]
        forward.append((count - 1, 0))
        backward = [(target, source) for source, target in forward]
        low = lax.ppermute(
            lax.slice_in_dim(block, block.shape[dim] - width, None, axis=dim), axis, forward
        )
        high = lax.ppermute(lax.slice_in_dim(block, 0, width, axis=dim), axis, backward)
        block = jnp.concatenate([low, block, high], axis=dim)
    return block


def turn_blocks(edge_row, width):
    lead = edge_row.shape[:-1]
    return edge_row.reshape(lead + (-1, width))[..., ::-1].reshape(edge_row.shape)


def face_flags(edge_flip):
    position = lax.axis_index("face")
    faces = edge_flip.shape[0]
    return (edge_flip[position] == 1, edge_flip[(position + 1) % faces] == 1)


def tile_flags(flags):
    tiles = flags[0].shape[0]
    spot = lax.axis_index("tile") % tiles
    return (flags[0][spot], flags[1][spot])


def stencil(padded, flags, width):
    top_flag, bottom_flag = tile_flags(flags)
    left = padded[..., 1:-1, :-2]
    right = padded[..., 1:-1, 2:]
    upper = padded[..., :-2, 1:-1]
    lower = padded[..., 2:, 1:-1]
    top_row = upper[..., 0, :]
    upper = upper.at[..., 0, :].set(jnp.where(top_flag, turn_blocks(top_row, width), top_row))
    bottom_row = lower[..., -1, :]
    lower = lower.at[..., -1, :].set(
        jnp.where(bottom_flag, turn_blocks(bottom_row, width), bottom_row)
    )
    return -0.25 * (upper + lower + left + right)


def fine_apply(field, flags):
    padded = with_halo(field, (("face", 2), ("tile", 3)), 1)
    return stencil(padded, flags, field.shape[-1])


def coarse_apply(field, flags):
    padded = with_halo(field, (("face", 2), ("tile", 3)), 1)
    return stencil(padded, flags, field.shape[-1])


def coarse_terms(field, flags):
    first = coarse_apply(field, flags)
    second = 2.0 * coarse_apply(first, flags) - field
    return (first, second)


def coarse_adjoint(parts, flags):
    inner = coarse_apply(parts[2], flags)
    outer = coarse_apply(parts[1] + 2.0 * inner, flags)
    return parts[0] - parts[2] + outer


def on_device(
    maps,
    params,
    labels,
    edge_flip,
    fine_weight,
    coarse_weight,
    feature_weight,
    param_weight,
    out_weight,
):
    flags = face_flags(edge_flip)
    field0 = maps.astype(jnp.float32)
    first0 = fine_apply(field0, flags)
    second0 = 2.0 * fine_apply(first0, flags) - field0
    terms0 = jnp.stack([field0, first0, second0])
    pre0 = jnp.einsum("kio,kbirc->borc", fine_weight, terms0, precision=exact)
    act0 = jax.nn.softplus(pre0)
    nmaps, nchan, nrows, ncols = act0.shape
    field1 = act0.reshape(nmaps, nchan, nrows // 2, 2, ncols // 2, 2).mean(axis=(3, 5))
    first1, second1 = coarse_terms(field1, flags)
    terms1 = jnp.stack([field1, first1, second1])
    pre1 = jnp.einsum("kio,kbirc->borc", coarse_weight, terms1, precision=exact)
    act1 = jax.nn.softplus(pre1)
    pooled_count = nrows // 2 * lax.axis_size("face") * (ncols // 2) * lax.axis_size("tile")
    features = lax.psum(act1.sum(axis=(2, 3)), ("face", "tile")) / pooled_count
    hidden = jnp.tanh(
        jnp.dot(features, feature_weight, precision=exact)
        + jnp.dot(params, param_weight, precision=exact)
    )
    logits = jnp.dot(hidden, out_weight, precision=exact)
    dlogit = jax.nn.sigmoid(logits) - labels.astype(jnp.float32)
    dhidden = dlogit[:, None] * out_weight[None, :] * (1.0 - hidden * hidden)
    dfeatures = jnp.dot(dhidden, feature_weight.T, precision=exact)
    dpre1 = (dfeatures / pooled_count)[:, :, None, None] * jax.nn.sigmoid(pre1)
    grad_c = jnp.einsum("kbirc,borc->kio", terms1, dpre1, precision=exact)
    parts1 = jnp.einsum("kio,borc->kbirc", coarse_weight, dpre1, precision=exact)
    dfield1 = coarse_adjoint(parts1, flags)
    spread = jnp.broadcast_to(
        dfield1[:, :, :, None, :, None], (nmaps, nchan, nrows // 2, 2, ncols // 2, 2)
    ).reshape(pre0.shape)
    dpre0 = 0.25 * spread * jax.nn.sigmoid(pre0)
    grad_f = jnp.einsum("kbirc,borc->kio", terms0, dpre0, precision=exact)
    parts0 = jnp.einsum("kio,borc->kbirc", fine_weight, dpre0, precision=exact)
    inner0 = fine_apply(parts0[2], flags)
    outer0 = fine_apply(parts0[1] + 2.0 * inner0, flags)
    pixel_count = nrows * lax.axis_size("face") * ncols * lax.axis_size("tile")
    saliency = (parts0[0] - parts0[2] + outer0) * pixel_count
    grad_f, grad_c = lax.psum((grad_f, grad_c), ("face", "tile"))
    return (logits, saliency, grad_f, grad_c)


def solution(mesh):
    in_specs = (P(None, None, "face", "tile"), P(), P(), P(), P(), P(), P(), P(), P())
    out_specs = (P(), P(None, None, "face", "tile"), P(), P())
    return jax.shard_map(
        on_device, mesh=mesh, in_specs=in_specs, out_specs=out_specs, check_vma=False
    )
```

profile of v0, /device:TPU:1, one launch (start us, length us, event | category | flops | bytes accessed | tf_op | source)
XLA Modules:
  0.0 429.5 jit_solution(592526183360856192)
XLA Ops:
  1.6 4.0 collective-permute-start
  5.6 4.1 collective-permute-start.1
  12.0 6.0 %collective-permute-start.2 = (f32[4,4,18,1]{3,1,2,0:T(4,128)S(1)}, f32[4,4,18,1]{3,1,2,0:T(4,128)S(1)}, u32[]{:S(2)}, u32[]{:S(2)}) collective-permute-start(f32[4,4,18,1]{3,1,2,0:T(4,128)S(1)} %get-tuple-element.242), channel_id=1, source_target_pairs={{0,1},{1,2},{2,3},{3,4},{4,5},{5,6},{6,7},{7,8},{8,9},{9,10},{10,1... | collective-permute-start | bytes 3464 | tf_op jit(solution)/shard_map/ppermute | solution.py:15
  18.1 4.5 %collective-permute-start.3 = (f32[4,4,18,1]{3,1,2,0:T(4,128)S(1)}, f32[4,4,18,1]{3,1,2,0:T(4,128)S(1)}, u32[]{:S(2)}, u32[]{:S(2)}) collective-permute-start(f32[4,4,18,1]{3,1,2,0:T(4,128)S(1)} %get-tuple-element.243), channel_id=1, source_target_pairs={{1,0},{2,1},{3,2},{4,3},{5,4},{6,5},{7,6},{8,7},{9,8},{10,9},{11,1... | collective-permute-start | bytes 3464 | tf_op jit(solution)/shard_map/ppermute | solution.py:18
  22.8 1.3 select_dynamic-update-slice_fusion.14
  24.2 1.9 collective-permute-done.3
  26.3 2.6 collective-permute-start.4
  28.9 4.8 %collective-permute-start.5 = (f32[4,4,1,128]{3,1,2,0:T(4,128)S(1)}, f32[4,4,1,128]{3,1,2,0:T(4,128)S(1)}, u32[]{:S(2)}, u32[]{:S(2)}) collective-permute-start(f32[4,4,1,128]{3,1,2,0:T(4,128)S(1)} %get-tuple-element.255), channel_id=1, source_target_pairs={{64,0},{128,64},{192,128},{256,192},{320,256},{384,320},{448,384},... | collective-permute-start | bytes 24584 | tf_op jit(solution)/shard_map/ppermute | solution.py:18
  34.7 2.9 collective-permute-start.6
  37.6 6.9 %collective-permute-start.7 = (f32[4,4,18,1]{3,1,2,0:T(4,128)S(1)}, f32[4,4,18,1]{3,1,2,0:T(4,128)S(1)}, u32[]{:S(2)}, u32[]{:S(2)}) collective-permute-start(f32[4,4,18,1]{3,1,2,0:T(4,128)S(1)} %get-tuple-element.241), channel_id=1, source_target_pairs={{1,0},{2,1},{3,2},{4,3},{5,4},{6,5},{7,6},{8,7},{9,8},{10,9},{11,1... | collective-permute-start | bytes 3464 | tf_op jit(solution)/shard_map/ppermute | solution.py:18
  46.1 1.1 fusion.37
  47.2 1.7 compare_select_fusion.1
  49.0 2.6 copy.39
  51.6 5.6 %reduce_sum.18 = f32[4,16,8,64]{1,3,2,0:T(8,128)S(1)} reduce(f32[4,16,8,2,64,2]{1,5,4,3,2,0:T(2,128)} %bitcast.121, f32[]{:T(128)} %constant.422.clone.1), dimensions={3,5}, to_apply=%region_0.1 | reduce | flops 98304 | bytes 655364 | tf_op jit(solution)/shard_map/reduce_sum | solution.py:96
  57.6 2.5 collective-permute-start.8
  60.1 5.4 %collective-permute-start.9 = (f32[4,16,1,64]{3,1,2,0:T(8,128)S(1)}, f32[4,16,1,64]{3,1,2,0:T(8,128)S(1)}, u32[]{:S(2)}, u32[]{:S(2)}) collective-permute-start(f32[4,16,1,64]{3,1,2,0:T(8,128)S(1)} %get-tuple-element.235), channel_id=1, source_target_pairs={{64,0},{128,64},{192,128},{256,192},{320,256},{384,320},{448,384},... | collective-permute-start | bytes 49160 | tf_op jit(solution)/shard_map/ppermute | solution.py:18
  66.8 2.1 collective-permute-start.10
  68.8 9.0 %collective-permute-start.11 = (f32[4,16,10,1]{3,1,2,0:T(8,128)S(1)}, f32[4,16,10,1]{3,1,2,0:T(8,128)S(1)}, u32[]{:S(2)}, u32[]{:S(2)}) collective-permute-start(f32[4,16,10,1]{3,1,2,0:T(8,128)S(1)} %get-tuple-element.217), channel_id=1, source_target_pairs={{1,0},{2,1},{3,2},{4,3},{5,4},{6,5},{7,6},{8,7},{9,8},{10,9},{11,1... | collective-permute-start | bytes 7688 | tf_op jit(solution)/shard_map/ppermute | solution.py:18
  79.8 1.9 collective-permute-start.12
  81.7 6.2 %collective-permute-start.13 = (f32[4,16,1,64]{3,1,2,0:T(8,128)S(1)}, f32[4,16,1,64]{3,1,2,0:T(8,128)S(1)}, u32[]{:S(2)}, u32[]{:S(2)}) collective-permute-start(f32[4,16,1,64]{3,1,2,0:T(8,128)S(1)} %get-tuple-element.231), channel_id=1, source_target_pairs={{64,0},{128,64},{192,128},{256,192},{320,256},{384,320},{448,384},... | collective-permute-start | bytes 49160 | tf_op jit(solution)/shard_map/ppermute | solution.py:18
  89.1 2.0 collective-permute-start.14
  91.0 11.0 %collective-permute-start.15 = (f32[4,16,10,1]{3,1,2,0:T(8,128)S(1)}, f32[4,16,10,1]{3,1,2,0:T(8,128)S(1)}, u32[]{:S(2)}, u32[]{:S(2)}) collective-permute-start(f32[4,16,10,1]{3,1,2,0:T(8,128)S(1)} %get-tuple-element.215), channel_id=1, source_target_pairs={{1,0},{2,1},{3,2},{4,3},{5,4},{6,5},{7,6},{8,7},{9,8},{10,9},{11,1... | collective-permute-start | bytes 7688 | tf_op jit(solution)/shard_map/ppermute | solution.py:18
  105.7 115.2 %psum.21 = f32[4,32]{1,0:T(4,128)S(1)} all-reduce(f32[4,32]{1,0:T(4,128)S(1)} %get-tuple-element.266), channel_id=1, replica_groups=mesh['face'=8,'tile'=64] {'face','tile'}, use_global_device_ids=true, to_apply=%region_2.3 | all-reduce | flops 128 | bytes 1024 | tf_op jit(solution)/shard_map/psum | solution.py:102
  223.1 1.9 collective-permute-start.16
  225.0 5.5 %collective-permute-start.17 = (f32[4,16,1,64]{3,1,2,0:T(8,128)S(1)}, f32[4,16,1,64]{3,1,2,0:T(8,128)S(1)}, u32[]{:S(2)}, u32[]{:S(2)}) collective-permute-start(f32[4,16,1,64]{3,1,2,0:T(8,128)S(1)} %get-tuple-element.225), channel_id=1, source_target_pairs={{64,0},{128,64},{192,128},{256,192},{320,256},{384,320},{448,384},... | collective-permute-start | bytes 49160 | tf_op jit(solution)/shard_map/ppermute | solution.py:18
  232.4 4.7 %collective-permute-start.18 = (f32[4,16,10,1]{3,1,2,0:T(8,128)}, f32[4,16,10,1]{3,1,2,0:T(8,128)S(1)}, u32[]{:S(2)}, u32[]{:S(2)}) collective-permute-start(f32[4,16,10,1]{3,1,2,0:T(8,128)} %get-tuple-element.212), channel_id=1, source_target_pairs={{0,1},{1,2},{2,3},{3,4},{4,5},{5,6},{6,7},{7,8},{8,9},{9,10},{10,1... | collective-permute-start | bytes 7688 | tf_op jit(solution)/shard_map/ppermute | solution.py:15
  237.1 2.1 collective-permute-start.19
  241.4 8.2 %collective-permute-done.19 = f32[4,16,10,1]{3,1,2,0:T(8,128)S(1)} collective-permute-done((f32[4,16,10,1]{3,1,2,0:T(8,128)S(1)}, f32[4,16,10,1]{3,1,2,0:T(8,128)S(1)}, u32[]{:S(2)}, u32[]{:S(2)}) %collective-permute-start.19) | collective-permute-done | bytes 2592 | tf_op jit(solution)/shard_map/ppermute | solution.py:18
  249.9 1.9 collective-permute-start.20
  251.8 6.1 %collective-permute-start.21 = (f32[4,16,1,64]{3,1,2,0:T(8,128)S(1)}, f32[4,16,1,64]{3,1,2,0:T(8,128)S(1)}, u32[]{:S(2)}, u32[]{:S(2)}) collective-permute-start(f32[4,16,1,64]{3,1,2,0:T(8,128)S(1)} %get-tuple-element.221), channel_id=1, source_target_pairs={{64,0},{128,64},{192,128},{256,192},{320,256},{384,320},{448,384},... | collective-permute-start | bytes 49160 | tf_op jit(solution)/shard_map/ppermute | solution.py:18
  259.8 3.3 collective-permute-start.22
  263.1 1.9 collective-permute-start.23
  266.6 4.3 %collective-permute-done.22 = f32[4,16,10,1]{3,1,2,0:T(8,128)S(1)} collective-permute-done((f32[4,16,10,1]{3,1,2,0:T(8,128)}, f32[4,16,10,1]{3,1,2,0:T(8,128)S(1)}, u32[]{:S(2)}, u32[]{:S(2)}) %collective-permute-start.22) | collective-permute-done | bytes 2592 | tf_op jit(solution)/shard_map/ppermute | solution.py:15
  271.0 4.1 collective-permute-done.23
  275.7 4.0 broadcast_in_dim.2
  279.7 2.8 copy.45
  283.5 1.9 collective-permute-start.24
  285.4 5.5 %collective-permute-start.25 = (f32[4,4,1,128]{3,1,2,0:T(4,128)S(1)}, f32[4,4,1,128]{3,1,2,0:T(4,128)S(1)}, u32[]{:S(2)}, u32[]{:S(2)}) collective-permute-start(f32[4,4,1,128]{3,1,2,0:T(4,128)S(1)} %get-tuple-element.251), channel_id=1, source_target_pairs={{64,0},{128,64},{192,128},{256,192},{320,256},{384,320},{448,384},... | collective-permute-start | bytes 24584 | tf_op jit(solution)/shard_map/ppermute | solution.py:18
  292.1 3.0 collective-permute-start.26
  295.1 1.9 collective-permute-start.27
  298.7 4.3 %collective-permute-done.27 = f32[4,4,18,1]{3,1,2,0:T(4,128)S(1)} collective-permute-done((f32[4,4,18,1]{3,1,2,0:T(4,128)S(1)}, f32[4,4,18,1]{3,1,2,0:T(4,128)S(1)}, u32[]{:S(2)}, u32[]{:S(2)}) %collective-permute-start.27) | collective-permute-done | bytes 1184 | tf_op jit(solution)/shard_map/ppermute | solution.py:18
  303.3 1.9 collective-permute-start.28
  305.2 5.7 %collective-permute-start.29 = (f32[4,4,1,128]{3,1,2,0:T(4,128)S(1)}, f32[4,4,1,128]{3,1,2,0:T(4,128)S(1)}, u32[]{:S(2)}, u32[]{:S(2)}) collective-permute-start(f32[4,4,1,128]{3,1,2,0:T(4,128)S(1)} %get-tuple-element.247), channel_id=1, source_target_pairs={{64,0},{128,64},{192,128},{256,192},{320,256},{384,320},{448,384},... | collective-permute-start | bytes 24584 | tf_op jit(solution)/shard_map/ppermute | solution.py:18
  311.0 1.7 convolution_bitcast_fusion.5
  312.6 103.5 %all-reduce = (f32[3,4,16]{2,1,0:T(4,128)}, f32[3,16,32]{2,1,0:T(8,128)}) all-reduce(f32[3,4,16]{2,1,0:T(4,128)S(1)} %convolution_bitcast_fusion.5, f32[3,16,32]{2,1,0:T(8,128)S(1)} %convolution_bitcast_fusion.4), channel_id=1, replica_groups=mesh['face'=8,'tile'=64] {'face','tile'}, use_global_device_ids=true, to_apply=%region_3.4 | all-reduce | flops 1728 | bytes 13824 | tf_op jit(solution)/shard_map/psum | solution.py:125
  416.4 4.2 collective-permute-start.30
  420.6 1.9 collective-permute-start.31
  424.1 4.4 %collective-permute-done.31 = f32[4,4,18,1]{3,1,2,0:T(4,128)S(1)} collective-permute-done((f32[4,4,18,1]{3,1,2,0:T(4,128)S(1)}, f32[4,4,18,1]{3,1,2,0:T(4,128)S(1)}, u32[]{:S(2)}, u32[]{:S(2)}) %collective-permute-start.31) | collective-permute-done | bytes 1184 | tf_op jit(solution)/shard_map/ppermute | solution.py:18
  (145 shorter events, 31.6 us)
Async XLA Ops:
  0.6 104.0 %copy-start = (f32[3,16,32]{2,1,0:T(8,128)S(1)}, f32[3,16,32]{2,1,0:T(8,128)}, u32[]{:S(2)}) copy-start(f32[3,16,32]{2,1,0:T(8,128)} %param.46) | copy-start | bytes 18436
  0.6 46.6 %copy-start.12 = (f32[3,4,16]{2,1,0:T(4,128)S(1)}, f32[3,4,16]{2,1,0:T(4,128)}, u32[]{:S(2)}) copy-start(f32[3,4,16]{2,1,0:T(4,128)} %param.45) | copy-start | bytes 2308
  1.6 50.0 %copy-start.7 = (f32[1,4,4,16,128]{4,2,0,3,1:T(4,128)}, f32[1,4,4,16,128]{4,2,0,3,1:T(4,128)S(1)}, u32[]{:S(2)}) copy-start(f32[1,4,4,16,128]{4,2,0,3,1:T(4,128)S(1)} %get-tuple-element.260) | copy-start | bytes 393220
  1.6 10.3 %collective-permute-start = (f32[4,4,1,128]{3,1,2,0:T(4,128)S(1)}, f32[4,4,1,128]{3,1,2,0:T(4,128)S(1)}, u32[]{:S(2)}, u32[]{:S(2)}) collective-permute-start(f32[4,4,1,128]{3,1,2,0:T(4,128)S(1)} %get-tuple-element.258), channel_id=1, source_target_pairs={{0,64},{64,128},{128,192},{192,256},{256,320},{320,384},{384,448},... | collective-permute-start | bytes 24584 | tf_op jit(solution)/shard_map/ppermute | solution.py:15
  5.6 6.2 %collective-permute-start.1 = (f32[4,4,1,128]{3,1,2,0:T(4,128)S(1)}, f32[4,4,1,128]{3,1,2,0:T(4,128)S(1)}, u32[]{:S(2)}, u32[]{:S(2)}) collective-permute-start(f32[4,4,1,128]{3,1,2,0:T(4,128)S(1)} %get-tuple-element.259), channel_id=1, source_target_pairs={{64,0},{128,64},{192,128},{256,192},{320,256},{384,320},{448,384},... | collective-permute-start | bytes 24584 | tf_op jit(solution)/shard_map/ppermute | solution.py:18
  12.0 12.1 %collective-permute-start.2 = (f32[4,4,18,1]{3,1,2,0:T(4,128)S(1)}, f32[4,4,18,1]{3,1,2,0:T(4,128)S(1)}, u32[]{:S(2)}, u32[]{:S(2)}) collective-permute-start(f32[4,4,18,1]{3,1,2,0:T(4,128)S(1)} %get-tuple-element.242), channel_id=1, source_target_pairs={{0,1},{1,2},{2,3},{3,4},{4,5},{5,6},{6,7},{7,8},{8,9},{9,10},{10,1... | collective-permute-start | bytes 3464 | tf_op jit(solution)/shard_map/ppermute | solution.py:15
  18.1 8.0 %collective-permute-start.3 = (f32[4,4,18,1]{3,1,2,0:T(4,128)S(1)}, f32[4,4,18,1]{3,1,2,0:T(4,128)S(1)}, u32[]{:S(2)}, u32[]{:S(2)}) collective-permute-start(f32[4,4,18,1]{3,1,2,0:T(4,128)S(1)} %get-tuple-element.243), channel_id=1, source_target_pairs={{1,0},{2,1},{3,2},{4,3},{5,4},{6,5},{7,6},{8,7},{9,8},{10,9},{11,1... | collective-permute-start | bytes 3464 | tf_op jit(solution)/shard_map/ppermute | solution.py:18
  26.3 7.4 %collective-permute-start.4 = (f32[4,4,1,128]{3,1,2,0:T(4,128)S(1)}, f32[4,4,1,128]{3,1,2,0:T(4,128)S(1)}, u32[]{:S(2)}, u32[]{:S(2)}) collective-permute-start(f32[4,4,1,128]{3,1,2,0:T(4,128)S(1)} %get-tuple-element.254), channel_id=1, source_target_pairs={{0,64},{64,128},{128,192},{192,256},{256,320},{320,384},{384,448},... | collective-permute-start | bytes 24584 | tf_op jit(solution)/shard_map/ppermute | solution.py:15
  28.9 5.6 %collective-permute-start.5 = (f32[4,4,1,128]{3,1,2,0:T(4,128)S(1)}, f32[4,4,1,128]{3,1,2,0:T(4,128)S(1)}, u32[]{:S(2)}, u32[]{:S(2)}) collective-permute-start(f32[4,4,1,128]{3,1,2,0:T(4,128)S(1)} %get-tuple-element.255), channel_id=1, source_target_pairs={{64,0},{128,64},{192,128},{256,192},{320,256},{384,320},{448,384},... | collective-permute-start | bytes 24584 | tf_op jit(solution)/shard_map/ppermute | solution.py:18
  34.7 11.4 %collective-permute-start.6 = (f32[4,4,18,1]{3,1,2,0:T(4,128)S(1)}, f32[4,4,18,1]{3,1,2,0:T(4,128)S(1)}, u32[]{:S(2)}, u32[]{:S(2)}) collective-permute-start(f32[4,4,18,1]{3,1,2,0:T(4,128)S(1)} %get-tuple-element.240), channel_id=1, source_target_pairs={{0,1},{1,2},{2,3},{3,4},{4,5},{5,6},{6,7},{7,8},{8,9},{9,10},{10,1... | collective-permute-start | bytes 3464 | tf_op jit(solution)/shard_map/ppermute | solution.py:15
  37.6 8.5 %collective-permute-start.7 = (f32[4,4,18,1]{3,1,2,0:T(4,128)S(1)}, f32[4,4,18,1]{3,1,2,0:T(4,128)S(1)}, u32[]{:S(2)}, u32[]{:S(2)}) collective-permute-start(f32[4,4,18,1]{3,1,2,0:T(4,128)S(1)} %get-tuple-element.241), channel_id=1, source_target_pairs={{1,0},{2,1},{3,2},{4,3},{5,4},{6,5},{7,6},{8,7},{9,8},{10,9},{11,1... | collective-permute-start | bytes 3464 | tf_op jit(solution)/shard_map/ppermute | solution.py:18
  47.2 4.4 %copy-start.5 = (f32[1,4,4,16,128]{4,2,0,3,1:T(4,128)}, f32[1,4,4,16,128]{4,2,0,3,1:T(4,128)S(1)}, u32[]{:S(2)}) copy-start(f32[1,4,4,16,128]{4,2,0,3,1:T(4,128)S(1)} %fusion.37) | copy-start | bytes 393220
  57.6 8.0 %collective-permute-start.8 = (f32[4,16,1,64]{3,1,2,0:T(8,128)S(1)}, f32[4,16,1,64]{3,1,2,0:T(8,128)S(1)}, u32[]{:S(2)}, u32[]{:S(2)}) collective-permute-start(f32[4,16,1,64]{3,1,2,0:T(8,128)S(1)} %get-tuple-element.234), channel_id=1, source_target_pairs={{0,64},{64,128},{128,192},{192,256},{256,320},{320,384},{384,448},... | collective-permute-start | bytes 49160 | tf_op jit(solution)/shard_map/ppermute | solution.py:15
  60.1 6.4 %collective-permute-start.9 = (f32[4,16,1,64]{3,1,2,0:T(8,128)S(1)}, f32[4,16,1,64]{3,1,2,0:T(8,128)S(1)}, u32[]{:S(2)}, u32[]{:S(2)}) collective-permute-start(f32[4,16,1,64]{3,1,2,0:T(8,128)S(1)} %get-tuple-element.235), channel_id=1, source_target_pairs={{64,0},{128,64},{192,128},{256,192},{320,256},{384,320},{448,384},... | collective-permute-start | bytes 49160 | tf_op jit(solution)/shard_map/ppermute | solution.py:18
  66.8 12.6 %collective-permute-start.10 = (f32[4,16,10,1]{3,1,2,0:T(8,128)S(1)}, f32[4,16,10,1]{3,1,2,0:T(8,128)S(1)}, u32[]{:S(2)}, u32[]{:S(2)}) collective-permute-start(f32[4,16,10,1]{3,1,2,0:T(8,128)S(1)} %get-tuple-element.216), channel_id=1, source_target_pairs={{0,1},{1,2},{2,3},{3,4},{4,5},{5,6},{6,7},{7,8},{8,9},{9,10},{10,1... | collective-permute-start | bytes 7688 | tf_op jit(solution)/shard_map/ppermute | solution.py:15
  68.8 10.6 %collective-permute-start.11 = (f32[4,16,10,1]{3,1,2,0:T(8,128)S(1)}, f32[4,16,10,1]{3,1,2,0:T(8,128)S(1)}, u32[]{:S(2)}, u32[]{:S(2)}) collective-permute-start(f32[4,16,10,1]{3,1,2,0:T(8,128)S(1)} %get-tuple-element.217), channel_id=1, source_target_pairs={{1,0},{2,1},{3,2},{4,3},{5,4},{6,5},{7,6},{8,7},{9,8},{10,9},{11,1... | collective-permute-start | bytes 7688 | tf_op jit(solution)/shard_map/ppermute | solution.py:18
  79.7 141.2 %copy-start.9 = (f32[32,128]{1,0:T(8,128)S(1)}, f32[32,128]{1,0:T(8,128)}, u32[]{:S(2)}) copy-start(f32[32,128]{1,0:T(8,128)} %param.47) | copy-start | bytes 49156
  79.7 141.3 %copy-start.10 = (f32[4,2]{0,1:T(2,128)S(1)}, f32[4,2]{0,1:T(2,128)}, u32[]{:S(2)}) copy-start(f32[4,2]{0,1:T(2,128)} %param.42) | copy-start | bytes 100
  79.7 141.3 %copy-start.11 = (f32[2,128]{1,0:T(2,128)S(1)}, f32[2,128]{1,0:T(2,128)}, u32[]{:S(2)}) copy-start(f32[2,128]{1,0:T(2,128)} %param.48) | copy-start | bytes 3076
  79.7 141.5 %copy-start.13 = (s32[4]{0:T(128)S(1)}, s32[4]{0:T(128)}, u32[]{:S(2)}) copy-start(s32[4]{0:T(128)} %param.43) | copy-start | bytes 52
  79.8 141.5 %copy-start.14 = (f32[128]{0:T(128)S(1)}, f32[128]{0:T(128)}, u32[]{:S(2)}) copy-start(f32[128]{0:T(128)} %param.49) | copy-start | bytes 1540
  79.8 8.1 %collective-permute-start.12 = (f32[4,16,1,64]{3,1,2,0:T(8,128)S(1)}, f32[4,16,1,64]{3,1,2,0:T(8,128)S(1)}, u32[]{:S(2)}, u32[]{:S(2)}) collective-permute-start(f32[4,16,1,64]{3,1,2,0:T(8,128)S(1)} %get-tuple-element.230), channel_id=1, source_target_pairs={{0,64},{64,128},{128,192},{192,256},{256,320},{320,384},{384,448},... | collective-permute-start | bytes 49160 | tf_op jit(solution)/shard_map/ppermute | solution.py:15
  81.7 7.2 %collective-permute-start.13 = (f32[4,16,1,64]{3,1,2,0:T(8,128)S(1)}, f32[4,16,1,64]{3,1,2,0:T(8,128)S(1)}, u32[]{:S(2)}, u32[]{:S(2)}) collective-permute-start(f32[4,16,1,64]{3,1,2,0:T(8,128)S(1)} %get-tuple-element.231), channel_id=1, source_target_pairs={{64,0},{128,64},{192,128},{256,192},{320,256},{384,320},{448,384},... | collective-permute-start | bytes 49160 | tf_op jit(solution)/shard_map/ppermute | solution.py:18
  89.1 14.6 %collective-permute-start.14 = (f32[4,16,10,1]{3,1,2,0:T(8,128)S(1)}, f32[4,16,10,1]{3,1,2,0:T(8,128)S(1)}, u32[]{:S(2)}, u32[]{:S(2)}) collective-permute-start(f32[4,16,10,1]{3,1,2,0:T(8,128)S(1)} %get-tuple-element.214), channel_id=1, source_target_pairs={{0,1},{1,2},{2,3},{3,4},{4,5},{5,6},{6,7},{7,8},{8,9},{9,10},{10,1... | collective-permute-start | bytes 7688 | tf_op jit(solution)/shard_map/ppermute | solution.py:15
  91.0 12.6 %collective-permute-start.15 = (f32[4,16,10,1]{3,1,2,0:T(8,128)S(1)}, f32[4,16,10,1]{3,1,2,0:T(8,128)S(1)}, u32[]{:S(2)}, u32[]{:S(2)}) collective-permute-start(f32[4,16,10,1]{3,1,2,0:T(8,128)S(1)} %get-tuple-element.215), channel_id=1, source_target_pairs={{1,0},{2,1},{3,2},{4,3},{5,4},{6,5},{7,6},{8,7},{9,8},{10,9},{11,1... | collective-permute-start | bytes 7688 | tf_op jit(solution)/shard_map/ppermute | solution.py:18
  104.0 0.7 copy-start.1
  104.0 1.7 copy-start.3
  223.1 7.4 %collective-permute-start.16 = (f32[4,16,1,64]{3,1,2,0:T(8,128)S(1)}, f32[4,16,1,64]{3,1,2,0:T(8,128)S(1)}, u32[]{:S(2)}, u32[]{:S(2)}) collective-permute-start(f32[4,16,1,64]{3,1,2,0:T(8,128)S(1)} %get-tuple-element.224), channel_id=1, source_target_pairs={{0,64},{64,128},{128,192},{192,256},{256,320},{320,384},{384,448},... | collective-permute-start | bytes 49160 | tf_op jit(solution)/shard_map/ppermute | solution.py:15
  225.0 6.5 %collective-permute-start.17 = (f32[4,16,1,64]{3,1,2,0:T(8,128)S(1)}, f32[4,16,1,64]{3,1,2,0:T(8,128)S(1)}, u32[]{:S(2)}, u32[]{:S(2)}) collective-permute-start(f32[4,16,1,64]{3,1,2,0:T(8,128)S(1)} %get-tuple-element.225), channel_id=1, source_target_pairs={{64,0},{128,64},{192,128},{256,192},{320,256},{384,320},{448,384},... | collective-permute-start | bytes 49160 | tf_op jit(solution)/shard_map/ppermute | solution.py:18
  232.4 9.0 %collective-permute-start.18 = (f32[4,16,10,1]{3,1,2,0:T(8,128)}, f32[4,16,10,1]{3,1,2,0:T(8,128)S(1)}, u32[]{:S(2)}, u32[]{:S(2)}) collective-permute-start(f32[4,16,10,1]{3,1,2,0:T(8,128)} %get-tuple-element.212), channel_id=1, source_target_pairs={{0,1},{1,2},{2,3},{3,4},{4,5},{5,6},{6,7},{7,8},{8,9},{9,10},{10,1... | collective-permute-start | bytes 7688 | tf_op jit(solution)/shard_map/ppermute | solution.py:15
  237.1 12.5 %collective-permute-start.19 = (f32[4,16,10,1]{3,1,2,0:T(8,128)S(1)}, f32[4,16,10,1]{3,1,2,0:T(8,128)S(1)}, u32[]{:S(2)}, u32[]{:S(2)}) collective-permute-start(f32[4,16,10,1]{3,1,2,0:T(8,128)S(1)} %get-tuple-element.213), channel_id=1, source_target_pairs={{1,0},{2,1},{3,2},{4,3},{5,4},{6,5},{7,6},{8,7},{9,8},{10,9},{11,1... | collective-permute-start | bytes 7688 | tf_op jit(solution)/shard_map/ppermute | solution.py:18
  249.9 8.0 %collective-permute-start.20 = (f32[4,16,1,64]{3,1,2,0:T(8,128)S(1)}, f32[4,16,1,64]{3,1,2,0:T(8,128)S(1)}, u32[]{:S(2)}, u32[]{:S(2)}) collective-permute-start(f32[4,16,1,64]{3,1,2,0:T(8,128)S(1)} %get-tuple-element.220), channel_id=1, source_target_pairs={{0,64},{64,128},{128,192},{192,256},{256,320},{320,384},{384,448},... | collective-permute-start | bytes 49160 | tf_op jit(solution)/shard_map/ppermute | solution.py:15
  251.8 7.1 %collective-permute-start.21 = (f32[4,16,1,64]{3,1,2,0:T(8,128)S(1)}, f32[4,16,1,64]{3,1,2,0:T(8,128)S(1)}, u32[]{:S(2)}, u32[]{:S(2)}) collective-permute-start(f32[4,16,1,64]{3,1,2,0:T(8,128)S(1)} %get-tuple-element.221), channel_id=1, source_target_pairs={{64,0},{128,64},{192,128},{256,192},{320,256},{384,320},{448,384},... | collective-permute-start | bytes 49160 | tf_op jit(solution)/shard_map/ppermute | solution.py:18
  259.8 11.1 %collective-permute-start.22 = (f32[4,16,10,1]{3,1,2,0:T(8,128)}, f32[4,16,10,1]{3,1,2,0:T(8,128)S(1)}, u32[]{:S(2)}, u32[]{:S(2)}) collective-permute-start(f32[4,16,10,1]{3,1,2,0:T(8,128)} %get-tuple-element.210), channel_id=1, source_target_pairs={{0,1},{1,2},{2,3},{3,4},{4,5},{5,6},{6,7},{7,8},{8,9},{9,10},{10,1... | collective-permute-start | bytes 7688 | tf_op jit(solution)/shard_map/ppermute | solution.py:15
  263.1 11.9 %collective-permute-start.23 = (f32[4,16,10,1]{3,1,2,0:T(8,128)S(1)}, f32[4,16,10,1]{3,1,2,0:T(8,128)S(1)}, u32[]{:S(2)}, u32[]{:S(2)}) collective-permute-start(f32[4,16,10,1]{3,1,2,0:T(8,128)S(1)} %get-tuple-element.211), channel_id=1, source_target_pairs={{1,0},{2,1},{3,2},{4,3},{5,4},{6,5},{7,6},{8,7},{9,8},{10,9},{11,1... | collective-permute-start | bytes 7688 | tf_op jit(solution)/shard_map/ppermute | solution.py:18
  275.7 6.9 %copy-start.15 = (f32[4,16,16,128]{3,1,2,0:T(8,128)S(1)}, f32[4,16,16,128]{3,1,2,0:T(8,128)}, u32[]{:S(2)}) copy-start(f32[4,16,16,128]{3,1,2,0:T(8,128)} %get-tuple-element.265) | copy-start | bytes 1572868
  279.7 11.2 %copy-start.2 = (f32[1,4,16,8,64]{4,2,0,3,1:T(8,128)S(1)}, f32[1,4,16,8,64]{4,2,0,3,1:T(8,128)}, u32[]{:S(2)}) copy-start(f32[1,4,16,8,64]{4,2,0,3,1:T(8,128)} %copy-done.1) | copy-start | bytes 393220
  279.7 11.2 %copy-start.4 = (f32[1,4,16,8,64]{4,2,0,3,1:T(8,128)S(1)}, f32[1,4,16,8,64]{4,2,0,3,1:T(8,128)}, u32[]{:S(2)}) copy-start(f32[1,4,16,8,64]{4,2,0,3,1:T(8,128)} %copy-done.3) | copy-start | bytes 393220
  282.6 28.4 %copy-start.6 = (f32[1,4,4,16,128]{4,2,0,3,1:T(4,128)S(1)}, f32[1,4,4,16,128]{4,2,0,3,1:T(4,128)}, u32[]{:S(2)}) copy-start(f32[1,4,4,16,128]{4,2,0,3,1:T(4,128)} %copy-done.5) | copy-start | bytes 393220
  282.6 28.4 %copy-start.8 = (f32[1,4,4,16,128]{4,2,0,3,1:T(4,128)S(1)}, f32[1,4,4,16,128]{4,2,0,3,1:T(4,128)}, u32[]{:S(2)}) copy-start(f32[1,4,4,16,128]{4,2,0,3,1:T(4,128)} %copy-done.7) | copy-start | bytes 393220
  283.5 8.3 %collective-permute-start.24 = (f32[4,4,1,128]{3,1,2,0:T(4,128)S(1)}, f32[4,4,1,128]{3,1,2,0:T(4,128)S(1)}, u32[]{:S(2)}, u32[]{:S(2)}) collective-permute-start(f32[4,4,1,128]{3,1,2,0:T(4,128)S(1)} %get-tuple-element.250), channel_id=1, source_target_pairs={{0,64},{64,128},{128,192},{192,256},{256,320},{320,384},{384,448},... | collective-permute-start | bytes 24584 | tf_op jit(solution)/shard_map/ppermute | solution.py:15
  285.4 6.4 %collective-permute-start.25 = (f32[4,4,1,128]{3,1,2,0:T(4,128)S(1)}, f32[4,4,1,128]{3,1,2,0:T(4,128)S(1)}, u32[]{:S(2)}, u32[]{:S(2)}) collective-permute-start(f32[4,4,1,128]{3,1,2,0:T(4,128)S(1)} %get-tuple-element.251), channel_id=1, source_target_pairs={{64,0},{128,64},{192,128},{256,192},{320,256},{384,320},{448,384},... | collective-permute-start | bytes 24584 | tf_op jit(solution)/shard_map/ppermute | solution.py:18
  292.1 6.6 %collective-permute-start.26 = (f32[4,4,18,1]{3,1,2,0:T(4,128)S(1)}, f32[4,4,18,1]{3,1,2,0:T(4,128)S(1)}, u32[]{:S(2)}, u32[]{:S(2)}) collective-permute-start(f32[4,4,18,1]{3,1,2,0:T(4,128)S(1)} %get-tuple-element.238), channel_id=1, source_target_pairs={{0,1},{1,2},{2,3},{3,4},{4,5},{5,6},{6,7},{7,8},{8,9},{9,10},{10,1... | collective-permute-start | bytes 3464 | tf_op jit(solution)/shard_map/ppermute | solution.py:15
  295.1 8.0 %collective-permute-start.27 = (f32[4,4,18,1]{3,1,2,0:T(4,128)S(1)}, f32[4,4,18,1]{3,1,2,0:T(4,128)S(1)}, u32[]{:S(2)}, u32[]{:S(2)}) collective-permute-start(f32[4,4,18,1]{3,1,2,0:T(4,128)S(1)} %get-tuple-element.239), channel_id=1, source_target_pairs={{1,0},{2,1},{3,2},{4,3},{5,4},{6,5},{7,6},{8,7},{9,8},{10,9},{11,1... | collective-permute-start | bytes 3464 | tf_op jit(solution)/shard_map/ppermute | solution.py:18
  303.3 112.9 %collective-permute-start.28 = (f32[4,4,1,128]{3,1,2,0:T(4,128)S(1)}, f32[4,4,1,128]{3,1,2,0:T(4,128)S(1)}, u32[]{:S(2)}, u32[]{:S(2)}) collective-permute-start(f32[4,4,1,128]{3,1,2,0:T(4,128)S(1)} %get-tuple-element.246), channel_id=1, source_target_pairs={{0,64},{64,128},{128,192},{192,256},{256,320},{320,384},{384,448},... | collective-permute-start | bytes 24584 | tf_op jit(solution)/shard_map/ppermute | solution.py:15
  305.2 110.9 %collective-permute-start.29 = (f32[4,4,1,128]{3,1,2,0:T(4,128)S(1)}, f32[4,4,1,128]{3,1,2,0:T(4,128)S(1)}, u32[]{:S(2)}, u32[]{:S(2)}) collective-permute-start(f32[4,4,1,128]{3,1,2,0:T(4,128)S(1)} %get-tuple-element.247), channel_id=1, source_target_pairs={{64,0},{128,64},{192,128},{256,192},{320,256},{384,320},{448,384},... | collective-permute-start | bytes 24584 | tf_op jit(solution)/shard_map/ppermute | solution.py:18
  416.4 7.7 %collective-permute-start.30 = (f32[4,4,18,1]{3,1,2,0:T(4,128)S(1)}, f32[4,4,18,1]{3,1,2,0:T(4,128)S(1)}, u32[]{:S(2)}, u32[]{:S(2)}) collective-permute-start(f32[4,4,18,1]{3,1,2,0:T(4,128)S(1)} %get-tuple-element.236), channel_id=1, source_target_pairs={{0,1},{1,2},{2,3},{3,4},{4,5},{5,6},{6,7},{7,8},{8,9},{9,10},{10,1... | collective-permute-start | bytes 3464 | tf_op jit(solution)/shard_map/ppermute | solution.py:15
  420.6 8.0 %collective-permute-start.31 = (f32[4,4,18,1]{3,1,2,0:T(4,128)S(1)}, f32[4,4,18,1]{3,1,2,0:T(4,128)S(1)}, u32[]{:S(2)}, u32[]{:S(2)}) collective-permute-start(f32[4,4,18,1]{3,1,2,0:T(4,128)S(1)} %get-tuple-element.237), channel_id=1, source_target_pairs={{1,0},{2,1},{3,2},{4,3},{5,4},{6,5},{7,6},{8,7},{9,8},{10,9},{11,1... | collective-permute-start | bytes 3464 | tf_op jit(solution)/shard_map/ppermute | solution.py:18
where the time goes:
time: 431 us; the launch traced here: 429 us
  blocking collectives  219 us (51%)
  starting transfers between devices  129 us (30%)
  waiting for transfers between devices  32.8 us (8%)
  other arithmetic  21.7 us (5%)
  local copies, waits for them, and re-layouts  17.1 us (4%)
  matrix products  8.29 us (2%)
    psum x1, blocking collectives, on_device(): features = lax.psum(act1.sum(axis=(2, 3)), ('face', 'tile')) / pooled_count  115 us
    psum x1, blocking collectives, on_device(): grad_f, grad_c = lax.psum((grad_f, grad_c), ('face', 'tile'))  104 us
    ppermute x16, starting transfers between devices, with_halo(): lax.ppermute(lax.slice_in_dim(block, 0, width, axis=dim), axis, backward)  82.5 us
    ppermute x16, starting transfers between devices, with_halo(): lax.ppermute(lax.slice_in_dim(block, block.shape[dim] - width, None, axis...  46.8 us
    ppermute x16, waiting for transfers between devices, with_halo(): lax.ppermute(lax.slice_in_dim(block, 0, width, axis=dim), axis, backward)  27.6 us
  transfers between devices with their start and end apart: 32, of which 13 were waited for; matrix products, arithmetic and copies ran while one was open for 4% of the time, Pallas kernels for 0%

commit v1 on v0

--- a/solution.py
+++ b/solution.py
@@ -99,7 +99,13 @@
     pre1 = jnp.einsum("kio,kbirc->borc", coarse_weight, terms1, precision=exact)
     act1 = jax.nn.softplus(pre1)
     pooled_count = nrows // 2 * lax.axis_size("face") * (ncols // 2) * lax.axis_size("tile")
-    features = lax.psum(act1.sum(axis=(2, 3)), ("face", "tile")) / pooled_count
+
+    def _number_ladders(xs, mesh_dim, net_axis):
+        for nth in (mesh_dim, net_axis):
+            xs = jax.lax.psum(xs, nth)
+        return xs
+
+    features = _number_ladders(act1.sum(axis=(2, 3)), "face", "tile") / pooled_count
     hidden = jnp.tanh(
         jnp.dot(features, feature_weight, precision=exact)
         + jnp.dot(params, param_weight, precision=exact)

time: 431 us -> 476 us (1.10)
  blocking collectives: 219 us -> 262 us
    psum x1 -> x2, blocking collectives: 115 us -> 157 us  [_number_ladders(): xs = jax.lax.psum(xs, nth)]
  transfers between devices with their start and end apart: 32 -> 32, of which waited for: 13 -> 12; matrix products, arithmetic and copies ran while one was open for 4% -> 3% of each run, Pallas kernels for 0% -> 0%
where the time goes in v1:
time: 476 us; the launch traced here: 475 us
  blocking collectives  262 us (55%)
  starting transfers between devices  131 us (28%)
  waiting for transfers between devices  33.2 us (7%)
  other arithmetic  21.2 us (4%)
  local copies, waits for them, and re-layouts  16.9 us (4%)
  matrix products  8.29 us (2%)
    psum x2, blocking collectives, _number_ladders(): xs = jax.lax.psum(xs, nth)  157 us
    psum x1, blocking collectives, on_device(): grad_f, grad_c = lax.psum((grad_f, grad_c), ('face', 'tile'))  105 us
    ppermute x16, starting transfers between devices, with_halo(): lax.ppermute(lax.slice_in_dim(block, 0, width, axis=dim), axis, backward)  85.9 us
    ppermute x16, starting transfers between devices, with_halo(): lax.ppermute(lax.slice_in_dim(block, block.shape[dim] - width, None, axis...  45.5 us
    ppermute x16, waiting for transfers between devices, with_halo(): lax.ppermute(lax.slice_in_dim(block, 0, width, axis=dim), axis, backward)  29.5 us
  transfers between devices with their start and end apart: 32, of which 12 were waited for; matrix products, arithmetic and copies ran while one was open for 3% of the time, Pallas kernels for 0%

profile of v1, /device:TPU:1, one launch (start us, length us, event | category | flops | bytes accessed | tf_op | source)
XLA Modules:
  0.0 475.0 jit_solution(2168950222777146546)
XLA Ops:
  1.6 4.0 collective-permute-start
  5.6 4.1 collective-permute-start.1
  11.9 6.0 %collective-permute-start.2 = (f32[4,4,18,1]{3,1,2,0:T(4,128)S(1)}, f32[4,4,18,1]{3,1,2,0:T(4,128)S(1)}, u32[]{:S(2)}, u32[]{:S(2)}) collective-permute-start(f32[4,4,18,1]{3,1,2,0:T(4,128)S(1)} %get-tuple-element.242), channel_id=1, source_target_pairs={{0,1},{1,2},{2,3},{3,4},{4,5},{5,6},{6,7},{7,8},{8,9},{9,10},{10,1... | collective-permute-start | bytes 3464 | tf_op jit(solution)/shard_map/ppermute | solution.py:15
  18.0 4.5 collective-permute-start.3
  24.0 1.9 collective-permute-done.3
  26.2 2.7 collective-permute-start.4
  28.9 4.7 collective-permute-start.5
  34.6 2.9 collective-permute-start.6
  37.5 6.9 %collective-permute-start.7 = (f32[4,4,18,1]{3,1,2,0:T(4,128)S(1)}, f32[4,4,18,1]{3,1,2,0:T(4,128)S(1)}, u32[]{:S(2)}, u32[]{:S(2)}) collective-permute-start(f32[4,4,18,1]{3,1,2,0:T(4,128)S(1)} %get-tuple-element.241), channel_id=1, source_target_pairs={{1,0},{2,1},{3,2},{4,3},{5,4},{6,5},{7,6},{8,7},{9,8},{10,9},{11,1... | collective-permute-start | bytes 3464 | tf_op jit(solution)/shard_map/ppermute | solution.py:18
  47.1 1.7 compare_select_fusion.1
  48.8 2.6 copy.39
  51.4 5.6 %reduce_sum.18 = f32[4,16,8,64]{1,3,2,0:T(8,128)S(1)} reduce(f32[4,16,8,2,64,2]{1,5,4,3,2,0:T(2,128)} %bitcast.121, f32[]{:T(128)} %constant.422.clone.1), dimensions={3,5}, to_apply=%region_0.1 | reduce | flops 98304 | bytes 655364 | tf_op jit(solution)/shard_map/reduce_sum | solution.py:96
  57.4 2.5 collective-permute-start.8
  60.0 5.4 %collective-permute-start.9 = (f32[4,16,1,64]{3,1,2,0:T(8,128)S(1)}, f32[4,16,1,64]{3,1,2,0:T(8,128)S(1)}, u32[]{:S(2)}, u32[]{:S(2)}) collective-permute-start(f32[4,16,1,64]{3,1,2,0:T(8,128)S(1)} %get-tuple-element.235), channel_id=1, source_target_pairs={{64,0},{128,64},{192,128},{256,192},{320,256},{384,320},{448,384},... | collective-permute-start | bytes 49160 | tf_op jit(solution)/shard_map/ppermute | solution.py:18
  66.6 2.1 collective-permute-start.10
  68.7 9.0 %collective-permute-start.11 = (f32[4,16,10,1]{3,1,2,0:T(8,128)S(1)}, f32[4,16,10,1]{3,1,2,0:T(8,128)S(1)}, u32[]{:S(2)}, u32[]{:S(2)}) collective-permute-start(f32[4,16,10,1]{3,1,2,0:T(8,128)S(1)} %get-tuple-element.217), channel_id=1, source_target_pairs={{1,0},{2,1},{3,2},{4,3},{5,4},{6,5},{7,6},{8,7},{9,8},{10,9},{11,1... | collective-permute-start | bytes 7688 | tf_op jit(solution)/shard_map/ppermute | solution.py:18
  79.6 1.9 collective-permute-start.12
  81.5 6.2 %collective-permute-start.13 = (f32[4,16,1,64]{3,1,2,0:T(8,128)S(1)}, f32[4,16,1,64]{3,1,2,0:T(8,128)S(1)}, u32[]{:S(2)}, u32[]{:S(2)}) collective-permute-start(f32[4,16,1,64]{3,1,2,0:T(8,128)S(1)} %get-tuple-element.231), channel_id=1, source_target_pairs={{64,0},{128,64},{192,128},{256,192},{320,256},{384,320},{448,384},... | collective-permute-start | bytes 49160 | tf_op jit(solution)/shard_map/ppermute | solution.py:18
  88.9 2.0 collective-permute-start.14
  90.9 11.1 %collective-permute-start.15 = (f32[4,16,10,1]{3,1,2,0:T(8,128)S(1)}, f32[4,16,10,1]{3,1,2,0:T(8,128)S(1)}, u32[]{:S(2)}, u32[]{:S(2)}) collective-permute-start(f32[4,16,10,1]{3,1,2,0:T(8,128)S(1)} %get-tuple-element.215), channel_id=1, source_target_pairs={{1,0},{2,1},{3,2},{4,3},{5,4},{6,5},{7,6},{8,7},{9,8},{10,9},{11,1... | collective-permute-start | bytes 7688 | tf_op jit(solution)/shard_map/ppermute | solution.py:18
  105.6 16.6 %psum.28 = f32[4,32]{1,0:T(4,128)S(1)} all-reduce(f32[4,32]{1,0:T(4,128)S(1)} %get-tuple-element.266), channel_id=1, replica_groups=mesh['face'=8,'tile'=64] {'face'}, use_global_device_ids=true, to_apply=%region_2.3 | all-reduce | flops 128 | bytes 1024 | tf_op jit(solution)/shard_map/psum | solution.py:105
  122.2 140.2 %psum.29 = f32[4,32]{1,0:T(4,128)S(1)} all-reduce(f32[4,32]{1,0:T(4,128)S(1)} %psum.28), channel_id=1, replica_groups=mesh['face'=8,'tile'=64] {'tile'}, use_global_device_ids=true, to_apply=%region_3.4 | all-reduce | flops 128 | bytes 1024 | tf_op jit(solution)/shard_map/psum | solution.py:105
  264.6 1.9 collective-permute-start.16
  266.5 5.5 %collective-permute-start.17 = (f32[4,16,1,64]{3,1,2,0:T(8,128)S(1)}, f32[4,16,1,64]{3,1,2,0:T(8,128)S(1)}, u32[]{:S(2)}, u32[]{:S(2)}) collective-permute-start(f32[4,16,1,64]{3,1,2,0:T(8,128)S(1)} %get-tuple-element.225), channel_id=1, source_target_pairs={{64,0},{128,64},{192,128},{256,192},{320,256},{384,320},{448,384},... | collective-permute-start | bytes 49160 | tf_op jit(solution)/shard_map/ppermute | solution.py:18
  273.9 3.3 collective-permute-start.18
  277.2 4.7 collective-permute-start.19
  283.4 1.7 collective-permute-done.18
  285.1 5.9 %collective-permute-done.19 = f32[4,16,10,1]{3,1,2,0:T(8,128)S(1)} collective-permute-done((f32[4,16,10,1]{3,1,2,0:T(8,128)S(1)}, f32[4,16,10,1]{3,1,2,0:T(8,128)S(1)}, u32[]{:S(2)}, u32[]{:S(2)}) %collective-permute-start.19) | collective-permute-done | bytes 2592 | tf_op jit(solution)/shard_map/ppermute | solution.py:18
  291.3 1.9 collective-permute-start.20
  293.2 5.7 %collective-permute-start.21 = (f32[4,16,1,64]{3,1,2,0:T(8,128)S(1)}, f32[4,16,1,64]{3,1,2,0:T(8,128)S(1)}, u32[]{:S(2)}, u32[]{:S(2)}) collective-permute-start(f32[4,16,1,64]{3,1,2,0:T(8,128)S(1)} %get-tuple-element.221), channel_id=1, source_target_pairs={{64,0},{128,64},{192,128},{256,192},{320,256},{384,320},{448,384},... | collective-permute-start | bytes 49160 | tf_op jit(solution)/shard_map/ppermute | solution.py:18
  300.6 3.2 collective-permute-start.22
  303.8 3.0 collective-permute-start.23
  308.3 1.9 collective-permute-done.22
  310.3 7.0 %collective-permute-done.23 = f32[4,16,10,1]{3,1,2,0:T(8,128)S(1)} collective-permute-done((f32[4,16,10,1]{3,1,2,0:T(8,128)S(1)}, f32[4,16,10,1]{3,1,2,0:T(8,128)S(1)}, u32[]{:S(2)}, u32[]{:S(2)}) %collective-permute-start.23) | collective-permute-done | bytes 2592 | tf_op jit(solution)/shard_map/ppermute | solution.py:18
  317.9 4.0 broadcast_in_dim.2
  321.9 2.8 copy.45
  325.7 1.9 collective-permute-start.24
  327.6 5.5 %collective-permute-start.25 = (f32[4,4,1,128]{3,1,2,0:T(4,128)S(1)}, f32[4,4,1,128]{3,1,2,0:T(4,128)S(1)}, u32[]{:S(2)}, u32[]{:S(2)}) collective-permute-start(f32[4,4,1,128]{3,1,2,0:T(4,128)S(1)} %get-tuple-element.251), channel_id=1, source_target_pairs={{64,0},{128,64},{192,128},{256,192},{320,256},{384,320},{448,384},... | collective-permute-start | bytes 24584 | tf_op jit(solution)/shard_map/ppermute | solution.py:18
  334.3 3.0 collective-permute-start.26
  337.3 1.9 collective-permute-start.27
  340.7 5.6 %collective-permute-done.27 = f32[4,4,18,1]{3,1,2,0:T(4,128)S(1)} collective-permute-done((f32[4,4,18,1]{3,1,2,0:T(4,128)S(1)}, f32[4,4,18,1]{3,1,2,0:T(4,128)S(1)}, u32[]{:S(2)}, u32[]{:S(2)}) %collective-permute-start.27) | collective-permute-done | bytes 1184 | tf_op jit(solution)/shard_map/ppermute | solution.py:18
  346.6 1.9 collective-permute-start.28
  348.6 6.0 %collective-permute-start.29 = (f32[4,4,1,128]{3,1,2,0:T(4,128)S(1)}, f32[4,4,1,128]{3,1,2,0:T(4,128)S(1)}, u32[]{:S(2)}, u32[]{:S(2)}) collective-permute-start(f32[4,4,1,128]{3,1,2,0:T(4,128)S(1)} %get-tuple-element.247), channel_id=1, source_target_pairs={{64,0},{128,64},{192,128},{256,192},{320,256},{384,320},{448,384},... | collective-permute-start | bytes 24584 | tf_op jit(solution)/shard_map/ppermute | solution.py:18
  354.6 1.7 convolution_bitcast_fusion.5
  356.2 105.4 %all-reduce = (f32[3,4,16]{2,1,0:T(4,128)}, f32[3,16,32]{2,1,0:T(8,128)}) all-reduce(f32[3,4,16]{2,1,0:T(4,128)S(1)} %convolution_bitcast_fusion.5, f32[3,16,32]{2,1,0:T(8,128)S(1)} %convolution_bitcast_fusion.4), channel_id=1, replica_groups=mesh['face'=8,'tile'=64] {'face','tile'}, use_global_device_ids=true, to_apply=%region_4.5 | all-reduce | flops 1728 | bytes 13824 | tf_op jit(solution)/shard_map/psum | solution.py:131
  461.8 4.2 collective-permute-start.30
  466.1 1.9 collective-permute-start.31
  469.5 4.5 collective-permute-done.31
  (146 shorter events, 32.5 us)
Async XLA Ops:
  0.6 103.9 %copy-start = (f32[3,16,32]{2,1,0:T(8,128)S(1)}, f32[3,16,32]{2,1,0:T(8,128)}, u32[]{:S(2)}) copy-start(f32[3,16,32]{2,1,0:T(8,128)} %param.46) | copy-start | bytes 18436
  0.6 46.4 %copy-start.12 = (f32[3,4,16]{2,1,0:T(4,128)S(1)}, f32[3,4,16]{2,1,0:T(4,128)}, u32[]{:S(2)}) copy-start(f32[3,4,16]{2,1,0:T(4,128)} %param.45) | copy-start | bytes 2308
  1.6 49.9 %copy-start.7 = (f32[1,4,4,16,128]{4,2,0,3,1:T(4,128)}, f32[1,4,4,16,128]{4,2,0,3,1:T(4,128)S(1)}, u32[]{:S(2)}) copy-start(f32[1,4,4,16,128]{4,2,0,3,1:T(4,128)S(1)} %get-tuple-element.260) | copy-start | bytes 393220
  1.6 10.2 %collective-permute-start = (f32[4,4,1,128]{3,1,2,0:T(4,128)S(1)}, f32[4,4,1,128]{3,1,2,0:T(4,128)S(1)}, u32[]{:S(2)}, u32[]{:S(2)}) collective-permute-start(f32[4,4,1,128]{3,1,2,0:T(4,128)S(1)} %get-tuple-element.258), channel_id=1, source_target_pairs={{0,64},{64,128},{128,192},{192,256},{256,320},{320,384},{384,448},... | collective-permute-start | bytes 24584 | tf_op jit(solution)/shard_map/ppermute | solution.py:15
  5.6 6.1 %collective-permute-start.1 = (f32[4,4,1,128]{3,1,2,0:T(4,128)S(1)}, f32[4,4,1,128]{3,1,2,0:T(4,128)S(1)}, u32[]{:S(2)}, u32[]{:S(2)}) collective-permute-start(f32[4,4,1,128]{3,1,2,0:T(4,128)S(1)} %get-tuple-element.259), channel_id=1, source_target_pairs={{64,0},{128,64},{192,128},{256,192},{320,256},{384,320},{448,384},... | collective-permute-start | bytes 24584 | tf_op jit(solution)/shard_map/ppermute | solution.py:18
  11.9 12.1 %collective-permute-start.2 = (f32[4,4,18,1]{3,1,2,0:T(4,128)S(1)}, f32[4,4,18,1]{3,1,2,0:T(4,128)S(1)}, u32[]{:S(2)}, u32[]{:S(2)}) collective-permute-start(f32[4,4,18,1]{3,1,2,0:T(4,128)S(1)} %get-tuple-element.242), channel_id=1, source_target_pairs={{0,1},{1,2},{2,3},{3,4},{4,5},{5,6},{6,7},{7,8},{8,9},{9,10},{10,1... | collective-permute-start | bytes 3464 | tf_op jit(solution)/shard_map/ppermute | solution.py:15
  18.0 8.0 %collective-permute-start.3 = (f32[4,4,18,1]{3,1,2,0:T(4,128)S(1)}, f32[4,4,18,1]{3,1,2,0:T(4,128)S(1)}, u32[]{:S(2)}, u32[]{:S(2)}) collective-permute-start(f32[4,4,18,1]{3,1,2,0:T(4,128)S(1)} %get-tuple-element.243), channel_id=1, source_target_pairs={{1,0},{2,1},{3,2},{4,3},{5,4},{6,5},{7,6},{8,7},{9,8},{10,9},{11,1... | collective-permute-start | bytes 3464 | tf_op jit(solution)/shard_map/ppermute | solution.py:18
  26.2 7.4 %collective-permute-start.4 = (f32[4,4,1,128]{3,1,2,0:T(4,128)S(1)}, f32[4,4,1,128]{3,1,2,0:T(4,128)S(1)}, u32[]{:S(2)}, u32[]{:S(2)}) collective-permute-start(f32[4,4,1,128]{3,1,2,0:T(4,128)S(1)} %get-tuple-element.254), channel_id=1, source_target_pairs={{0,64},{64,128},{128,192},{192,256},{256,320},{320,384},{384,448},... | collective-permute-start | bytes 24584 | tf_op jit(solution)/shard_map/ppermute | solution.py:15
  28.9 5.5 %collective-permute-start.5 = (f32[4,4,1,128]{3,1,2,0:T(4,128)S(1)}, f32[4,4,1,128]{3,1,2,0:T(4,128)S(1)}, u32[]{:S(2)}, u32[]{:S(2)}) collective-permute-start(f32[4,4,1,128]{3,1,2,0:T(4,128)S(1)} %get-tuple-element.255), channel_id=1, source_target_pairs={{64,0},{128,64},{192,128},{256,192},{320,256},{384,320},{448,384},... | collective-permute-start | bytes 24584 | tf_op jit(solution)/shard_map/ppermute | solution.py:18
  34.6 11.3 %collective-permute-start.6 = (f32[4,4,18,1]{3,1,2,0:T(4,128)S(1)}, f32[4,4,18,1]{3,1,2,0:T(4,128)S(1)}, u32[]{:S(2)}, u32[]{:S(2)}) collective-permute-start(f32[4,4,18,1]{3,1,2,0:T(4,128)S(1)} %get-tuple-element.240), channel_id=1, source_target_pairs={{0,1},{1,2},{2,3},{3,4},{4,5},{5,6},{6,7},{7,8},{8,9},{9,10},{10,1... | collective-permute-start | bytes 3464 | tf_op jit(solution)/shard_map/ppermute | solution.py:15
  37.5 8.4 %collective-permute-start.7 = (f32[4,4,18,1]{3,1,2,0:T(4,128)S(1)}, f32[4,4,18,1]{3,1,2,0:T(4,128)S(1)}, u32[]{:S(2)}, u32[]{:S(2)}) collective-permute-start(f32[4,4,18,1]{3,1,2,0:T(4,128)S(1)} %get-tuple-element.241), channel_id=1, source_target_pairs={{1,0},{2,1},{3,2},{4,3},{5,4},{6,5},{7,6},{8,7},{9,8},{10,9},{11,1... | collective-permute-start | bytes 3464 | tf_op jit(solution)/shard_map/ppermute | solution.py:18
  47.0 4.4 copy-start.5
  57.4 8.0 %collective-permute-start.8 = (f32[4,16,1,64]{3,1,2,0:T(8,128)S(1)}, f32[4,16,1,64]{3,1,2,0:T(8,128)S(1)}, u32[]{:S(2)}, u32[]{:S(2)}) collective-permute-start(f32[4,16,1,64]{3,1,2,0:T(8,128)S(1)} %get-tuple-element.234), channel_id=1, source_target_pairs={{0,64},{64,128},{128,192},{192,256},{256,320},{320,384},{384,448},... | collective-permute-start | bytes 49160 | tf_op jit(solution)/shard_map/ppermute | solution.py:15
  60.0 6.4 %collective-permute-start.9 = (f32[4,16,1,64]{3,1,2,0:T(8,128)S(1)}, f32[4,16,1,64]{3,1,2,0:T(8,128)S(1)}, u32[]{:S(2)}, u32[]{:S(2)}) collective-permute-start(f32[4,16,1,64]{3,1,2,0:T(8,128)S(1)} %get-tuple-element.235), channel_id=1, source_target_pairs={{64,0},{128,64},{192,128},{256,192},{320,256},{384,320},{448,384},... | collective-permute-start | bytes 49160 | tf_op jit(solution)/shard_map/ppermute | solution.py:18
  66.6 12.6 %collective-permute-start.10 = (f32[4,16,10,1]{3,1,2,0:T(8,128)S(1)}, f32[4,16,10,1]{3,1,2,0:T(8,128)S(1)}, u32[]{:S(2)}, u32[]{:S(2)}) collective-permute-start(f32[4,16,10,1]{3,1,2,0:T(8,128)S(1)} %get-tuple-element.216), channel_id=1, source_target_pairs={{0,1},{1,2},{2,3},{3,4},{4,5},{5,6},{6,7},{7,8},{8,9},{9,10},{10,1... | collective-permute-start | bytes 7688 | tf_op jit(solution)/shard_map/ppermute | solution.py:15
  68.7 10.5 %collective-permute-start.11 = (f32[4,16,10,1]{3,1,2,0:T(8,128)S(1)}, f32[4,16,10,1]{3,1,2,0:T(8,128)S(1)}, u32[]{:S(2)}, u32[]{:S(2)}) collective-permute-start(f32[4,16,10,1]{3,1,2,0:T(8,128)S(1)} %get-tuple-element.217), channel_id=1, source_target_pairs={{1,0},{2,1},{3,2},{4,3},{5,4},{6,5},{7,6},{8,7},{9,8},{10,9},{11,1... | collective-permute-start | bytes 7688 | tf_op jit(solution)/shard_map/ppermute | solution.py:18
  79.5 182.9 %copy-start.9 = (f32[32,128]{1,0:T(8,128)S(1)}, f32[32,128]{1,0:T(8,128)}, u32[]{:S(2)}) copy-start(f32[32,128]{1,0:T(8,128)} %param.47) | copy-start | bytes 49156
  79.5 183.0 %copy-start.10 = (f32[4,2]{0,1:T(2,128)S(1)}, f32[4,2]{0,1:T(2,128)}, u32[]{:S(2)}) copy-start(f32[4,2]{0,1:T(2,128)} %param.42) | copy-start | bytes 100
  79.6 183.0 %copy-start.11 = (f32[2,128]{1,0:T(2,128)S(1)}, f32[2,128]{1,0:T(2,128)}, u32[]{:S(2)}) copy-start(f32[2,128]{1,0:T(2,128)} %param.48) | copy-start | bytes 3076
  79.6 183.2 %copy-start.13 = (s32[4]{0:T(128)S(1)}, s32[4]{0:T(128)}, u32[]{:S(2)}) copy-start(s32[4]{0:T(128)} %param.43) | copy-start | bytes 52
  79.6 183.2 %copy-start.14 = (f32[128]{0:T(128)S(1)}, f32[128]{0:T(128)}, u32[]{:S(2)}) copy-start(f32[128]{0:T(128)} %param.49) | copy-start | bytes 1540
  79.6 8.1 %collective-permute-start.12 = (f32[4,16,1,64]{3,1,2,0:T(8,128)S(1)}, f32[4,16,1,64]{3,1,2,0:T(8,128)S(1)}, u32[]{:S(2)}, u32[]{:S(2)}) collective-permute-start(f32[4,16,1,64]{3,1,2,0:T(8,128)S(1)} %get-tuple-element.230), channel_id=1, source_target_pairs={{0,64},{64,128},{128,192},{192,256},{256,320},{320,384},{384,448},... | collective-permute-start | bytes 49160 | tf_op jit(solution)/shard_map/ppermute | solution.py:15
  81.5 7.2 %collective-permute-start.13 = (f32[4,16,1,64]{3,1,2,0:T(8,128)S(1)}, f32[4,16,1,64]{3,1,2,0:T(8,128)S(1)}, u32[]{:S(2)}, u32[]{:S(2)}) collective-permute-start(f32[4,16,1,64]{3,1,2,0:T(8,128)S(1)} %get-tuple-element.231), channel_id=1, source_target_pairs={{64,0},{128,64},{192,128},{256,192},{320,256},{384,320},{448,384},... | collective-permute-start | bytes 49160 | tf_op jit(solution)/shard_map/ppermute | solution.py:18
  88.9 14.6 %collective-permute-start.14 = (f32[4,16,10,1]{3,1,2,0:T(8,128)S(1)}, f32[4,16,10,1]{3,1,2,0:T(8,128)S(1)}, u32[]{:S(2)}, u32[]{:S(2)}) collective-permute-start(f32[4,16,10,1]{3,1,2,0:T(8,128)S(1)} %get-tuple-element.214), channel_id=1, source_target_pairs={{0,1},{1,2},{2,3},{3,4},{4,5},{5,6},{6,7},{7,8},{8,9},{9,10},{10,1... | collective-permute-start | bytes 7688 | tf_op jit(solution)/shard_map/ppermute | solution.py:15
  90.9 12.6 %collective-permute-start.15 = (f32[4,16,10,1]{3,1,2,0:T(8,128)S(1)}, f32[4,16,10,1]{3,1,2,0:T(8,128)S(1)}, u32[]{:S(2)}, u32[]{:S(2)}) collective-permute-start(f32[4,16,10,1]{3,1,2,0:T(8,128)S(1)} %get-tuple-element.215), channel_id=1, source_target_pairs={{1,0},{2,1},{3,2},{4,3},{5,4},{6,5},{7,6},{8,7},{9,8},{10,9},{11,1... | collective-permute-start | bytes 7688 | tf_op jit(solution)/shard_map/ppermute | solution.py:18
  103.8 0.7 copy-start.1
  103.8 1.8 copy-start.3
  264.6 7.4 %collective-permute-start.16 = (f32[4,16,1,64]{3,1,2,0:T(8,128)S(1)}, f32[4,16,1,64]{3,1,2,0:T(8,128)S(1)}, u32[]{:S(2)}, u32[]{:S(2)}) collective-permute-start(f32[4,16,1,64]{3,1,2,0:T(8,128)S(1)} %get-tuple-element.224), channel_id=1, source_target_pairs={{0,64},{64,128},{128,192},{192,256},{256,320},{320,384},{384,448},... | collective-permute-start | bytes 49160 | tf_op jit(solution)/shard_map/ppermute | solution.py:15
  266.5 6.5 %collective-permute-start.17 = (f32[4,16,1,64]{3,1,2,0:T(8,128)S(1)}, f32[4,16,1,64]{3,1,2,0:T(8,128)S(1)}, u32[]{:S(2)}, u32[]{:S(2)}) collective-permute-start(f32[4,16,1,64]{3,1,2,0:T(8,128)S(1)} %get-tuple-element.225), channel_id=1, source_target_pairs={{64,0},{128,64},{192,128},{256,192},{320,256},{384,320},{448,384},... | collective-permute-start | bytes 49160 | tf_op jit(solution)/shard_map/ppermute | solution.py:18
  273.9 11.1 %collective-permute-start.18 = (f32[4,16,10,1]{3,1,2,0:T(8,128)}, f32[4,16,10,1]{3,1,2,0:T(8,128)S(1)}, u32[]{:S(2)}, u32[]{:S(2)}) collective-permute-start(f32[4,16,10,1]{3,1,2,0:T(8,128)} %get-tuple-element.212), channel_id=1, source_target_pairs={{0,1},{1,2},{2,3},{3,4},{4,5},{5,6},{6,7},{7,8},{8,9},{9,10},{10,1... | collective-permute-start | bytes 7688 | tf_op jit(solution)/shard_map/ppermute | solution.py:15
  277.2 13.8 %collective-permute-start.19 = (f32[4,16,10,1]{3,1,2,0:T(8,128)S(1)}, f32[4,16,10,1]{3,1,2,0:T(8,128)S(1)}, u32[]{:S(2)}, u32[]{:S(2)}) collective-permute-start(f32[4,16,10,1]{3,1,2,0:T(8,128)S(1)} %get-tuple-element.213), channel_id=1, source_target_pairs={{1,0},{2,1},{3,2},{4,3},{5,4},{6,5},{7,6},{8,7},{9,8},{10,9},{11,1... | collective-permute-start | bytes 7688 | tf_op jit(solution)/shard_map/ppermute | solution.py:18
  291.3 7.6 %collective-permute-start.20 = (f32[4,16,1,64]{3,1,2,0:T(8,128)S(1)}, f32[4,16,1,64]{3,1,2,0:T(8,128)S(1)}, u32[]{:S(2)}, u32[]{:S(2)}) collective-permute-start(f32[4,16,1,64]{3,1,2,0:T(8,128)S(1)} %get-tuple-element.220), channel_id=1, source_target_pairs={{0,64},{64,128},{128,192},{192,256},{256,320},{320,384},{384,448},... | collective-permute-start | bytes 49160 | tf_op jit(solution)/shard_map/ppermute | solution.py:15
  293.2 6.5 %collective-permute-start.21 = (f32[4,16,1,64]{3,1,2,0:T(8,128)S(1)}, f32[4,16,1,64]{3,1,2,0:T(8,128)S(1)}, u32[]{:S(2)}, u32[]{:S(2)}) collective-permute-start(f32[4,16,1,64]{3,1,2,0:T(8,128)S(1)} %get-tuple-element.221), channel_id=1, source_target_pairs={{64,0},{128,64},{192,128},{256,192},{320,256},{384,320},{448,384},... | collective-permute-start | bytes 49160 | tf_op jit(solution)/shard_map/ppermute | solution.py:18
  300.6 9.6 %collective-permute-start.22 = (f32[4,16,10,1]{3,1,2,0:T(8,128)}, f32[4,16,10,1]{3,1,2,0:T(8,128)S(1)}, u32[]{:S(2)}, u32[]{:S(2)}) collective-permute-start(f32[4,16,10,1]{3,1,2,0:T(8,128)} %get-tuple-element.210), channel_id=1, source_target_pairs={{0,1},{1,2},{2,3},{3,4},{4,5},{5,6},{6,7},{7,8},{8,9},{9,10},{10,1... | collective-permute-start | bytes 7688 | tf_op jit(solution)/shard_map/ppermute | solution.py:15
  303.8 13.4 %collective-permute-start.23 = (f32[4,16,10,1]{3,1,2,0:T(8,128)S(1)}, f32[4,16,10,1]{3,1,2,0:T(8,128)S(1)}, u32[]{:S(2)}, u32[]{:S(2)}) collective-permute-start(f32[4,16,10,1]{3,1,2,0:T(8,128)S(1)} %get-tuple-element.211), channel_id=1, source_target_pairs={{1,0},{2,1},{3,2},{4,3},{5,4},{6,5},{7,6},{8,7},{9,8},{10,9},{11,1... | collective-permute-start | bytes 7688 | tf_op jit(solution)/shard_map/ppermute | solution.py:18
  317.9 6.9 %copy-start.15 = (f32[4,16,16,128]{3,1,2,0:T(8,128)S(1)}, f32[4,16,16,128]{3,1,2,0:T(8,128)}, u32[]{:S(2)}) copy-start(f32[4,16,16,128]{3,1,2,0:T(8,128)} %get-tuple-element.265) | copy-start | bytes 1572868
  321.9 11.2 %copy-start.2 = (f32[1,4,16,8,64]{4,2,0,3,1:T(8,128)S(1)}, f32[1,4,16,8,64]{4,2,0,3,1:T(8,128)}, u32[]{:S(2)}) copy-start(f32[1,4,16,8,64]{4,2,0,3,1:T(8,128)} %copy-done.1) | copy-start | bytes 393220
  321.9 11.2 %copy-start.4 = (f32[1,4,16,8,64]{4,2,0,3,1:T(8,128)S(1)}, f32[1,4,16,8,64]{4,2,0,3,1:T(8,128)}, u32[]{:S(2)}) copy-start(f32[1,4,16,8,64]{4,2,0,3,1:T(8,128)} %copy-done.3) | copy-start | bytes 393220
  324.8 29.8 %copy-start.6 = (f32[1,4,4,16,128]{4,2,0,3,1:T(4,128)S(1)}, f32[1,4,4,16,128]{4,2,0,3,1:T(4,128)}, u32[]{:S(2)}) copy-start(f32[1,4,4,16,128]{4,2,0,3,1:T(4,128)} %copy-done.5) | copy-start | bytes 393220
  324.8 29.8 %copy-start.8 = (f32[1,4,4,16,128]{4,2,0,3,1:T(4,128)S(1)}, f32[1,4,4,16,128]{4,2,0,3,1:T(4,128)}, u32[]{:S(2)}) copy-start(f32[1,4,4,16,128]{4,2,0,3,1:T(4,128)} %copy-done.7) | copy-start | bytes 393220
  325.7 8.3 %collective-permute-start.24 = (f32[4,4,1,128]{3,1,2,0:T(4,128)S(1)}, f32[4,4,1,128]{3,1,2,0:T(4,128)S(1)}, u32[]{:S(2)}, u32[]{:S(2)}) collective-permute-start(f32[4,4,1,128]{3,1,2,0:T(4,128)S(1)} %get-tuple-element.250), channel_id=1, source_target_pairs={{0,64},{64,128},{128,192},{192,256},{256,320},{320,384},{384,448},... | collective-permute-start | bytes 24584 | tf_op jit(solution)/shard_map/ppermute | solution.py:15
  327.6 6.4 %collective-permute-start.25 = (f32[4,4,1,128]{3,1,2,0:T(4,128)S(1)}, f32[4,4,1,128]{3,1,2,0:T(4,128)S(1)}, u32[]{:S(2)}, u32[]{:S(2)}) collective-permute-start(f32[4,4,1,128]{3,1,2,0:T(4,128)S(1)} %get-tuple-element.251), channel_id=1, source_target_pairs={{64,0},{128,64},{192,128},{256,192},{320,256},{384,320},{448,384},... | collective-permute-start | bytes 24584 | tf_op jit(solution)/shard_map/ppermute | solution.py:18
  334.3 6.5 %collective-permute-start.26 = (f32[4,4,18,1]{3,1,2,0:T(4,128)S(1)}, f32[4,4,18,1]{3,1,2,0:T(4,128)S(1)}, u32[]{:S(2)}, u32[]{:S(2)}) collective-permute-start(f32[4,4,18,1]{3,1,2,0:T(4,128)S(1)} %get-tuple-element.238), channel_id=1, source_target_pairs={{0,1},{1,2},{2,3},{3,4},{4,5},{5,6},{6,7},{7,8},{8,9},{9,10},{10,1... | collective-permute-start | bytes 3464 | tf_op jit(solution)/shard_map/ppermute | solution.py:15
  337.3 9.1 %collective-permute-start.27 = (f32[4,4,18,1]{3,1,2,0:T(4,128)S(1)}, f32[4,4,18,1]{3,1,2,0:T(4,128)S(1)}, u32[]{:S(2)}, u32[]{:S(2)}) collective-permute-start(f32[4,4,18,1]{3,1,2,0:T(4,128)S(1)} %get-tuple-element.239), channel_id=1, source_target_pairs={{1,0},{2,1},{3,2},{4,3},{5,4},{6,5},{7,6},{8,7},{9,8},{10,9},{11,1... | collective-permute-start | bytes 3464 | tf_op jit(solution)/shard_map/ppermute | solution.py:18
  346.6 115.0 %collective-permute-start.28 = (f32[4,4,1,128]{3,1,2,0:T(4,128)S(1)}, f32[4,4,1,128]{3,1,2,0:T(4,128)S(1)}, u32[]{:S(2)}, u32[]{:S(2)}) collective-permute-start(f32[4,4,1,128]{3,1,2,0:T(4,128)S(1)} %get-tuple-element.246), channel_id=1, source_target_pairs={{0,64},{64,128},{128,192},{192,256},{256,320},{320,384},{384,448},... | collective-permute-start | bytes 24584 | tf_op jit(solution)/shard_map/ppermute | solution.py:15
  348.6 113.1 %collective-permute-start.29 = (f32[4,4,1,128]{3,1,2,0:T(4,128)S(1)}, f32[4,4,1,128]{3,1,2,0:T(4,128)S(1)}, u32[]{:S(2)}, u32[]{:S(2)}) collective-permute-start(f32[4,4,1,128]{3,1,2,0:T(4,128)S(1)} %get-tuple-element.247), channel_id=1, source_target_pairs={{64,0},{128,64},{192,128},{256,192},{320,256},{384,320},{448,384},... | collective-permute-start | bytes 24584 | tf_op jit(solution)/shard_map/ppermute | solution.py:18
  461.8 7.7 %collective-permute-start.30 = (f32[4,4,18,1]{3,1,2,0:T(4,128)S(1)}, f32[4,4,18,1]{3,1,2,0:T(4,128)S(1)}, u32[]{:S(2)}, u32[]{:S(2)}) collective-permute-start(f32[4,4,18,1]{3,1,2,0:T(4,128)S(1)} %get-tuple-element.236), channel_id=1, source_target_pairs={{0,1},{1,2},{2,3},{3,4},{4,5},{5,6},{6,7},{7,8},{8,9},{9,10},{10,1... | collective-permute-start | bytes 3464 | tf_op jit(solution)/shard_map/ppermute | solution.py:15
  466.1 8.0 %collective-permute-start.31 = (f32[4,4,18,1]{3,1,2,0:T(4,128)S(1)}, f32[4,4,18,1]{3,1,2,0:T(4,128)S(1)}, u32[]{:S(2)}, u32[]{:S(2)}) collective-permute-start(f32[4,4,18,1]{3,1,2,0:T(4,128)S(1)} %get-tuple-element.237), channel_id=1, source_target_pairs={{1,0},{2,1},{3,2},{4,3},{5,4},{6,5},{7,6},{8,7},{9,8},{10,9},{11,1... | collective-permute-start | bytes 3464 | tf_op jit(solution)/shard_map/ppermute | solution.py:18
